TPU v7x, 512 devices: a whole 4x4x16 slice. The times are simulated.
512 devices in a mesh: sub: 64 (over z_lo, y, core), strip: 8 (over x, z_hi).
Axes of the slice: x: 4, y: 4, z: 16 (z_hi: 2, z_lo: 8; z = z_hi * 8 + z_lo), core: 2. Of those that a mesh axis runs over, the one named last changes fastest.
Arguments:
- spectra: bfloat16 [128, 256, 2048], P('sub', 'strip'), may hold values from -6 to 6
- offsets: int32 [128], P('sub'), may hold values from 0 to 1023
Outputs:
- foreground: float32 [1024, 256, 128], P('strip', 'sub')
All inputs are finite; a program needn't handle non-finite values.
Results may differ from a plain program's by a relative error of at most 0.0068.
Values may be sent and summed in bfloat16 or wider, within the bound.
No kernel may reach another device: no remote copies, remote signals or barrier semaphores. Data moves between devices by JAX's collectives and lax.ppermute only.
A program may use at most 64 MiB of HBM per device.

v0:
```python
import math
import jax
import jax.numpy as jnp
import numpy as np
from jax import lax
from jax.sharding import PartitionSpec as P

KR = 256
ROWS = 1024
COLS = 256
WIN = 8
BG = 16


def from_behind(value, axis, steps):
    count = lax.axis_size(axis)
    pairs = [(source, (source + steps) % count) for source in range(count)]
    return lax.ppermute(value, axis, pairs)


def extended(shard, sides, width):
    for axis, dim in sides:
        count, length = (lax.axis_size(axis), shard.shape[dim])
        up = [(i, (i + 1) % count) for i in range(count - 1)]
        down = [(j, i) for i, j in up]
        last = lax.slice_in_dim(shard, length - width, length, axis=dim)
        leading = lax.slice_in_dim(shard, 0, width, axis=dim)
        before = lax.ppermute(last, axis, up)
        after = lax.ppermute(leading, axis, down)
        shard = jnp.concatenate([before, shard, after], axis=dim)
    return shard


def column_table(samples, width):
    sample_index = jnp.arange(samples, dtype=jnp.int32)[:, None]
    column_index = jnp.arange(width, dtype=jnp.int32)[None, :]
    phase = jnp.mod(sample_index * column_index, samples).astype(jnp.float32) * (
        2.0 * math.pi / samples
    )
    cosine = jnp.cos(phase) / math.sqrt(samples)
    sine = -jnp.sin(phase) / math.sqrt(samples)
    upper = jnp.concatenate([cosine, sine], axis=1)
    lower = jnp.concatenate([-sine, cosine], axis=1)
    return jnp.concatenate([upper, lower], axis=0).astype(jnp.bfloat16)


def row_table(row_index, samples, image_rows):
    sample_index = jnp.arange(samples, dtype=jnp.int32)[None, :] - samples // 2
    phase = jnp.mod(row_index[:, None] * sample_index, image_rows).astype(jnp.float32) * (
        2.0 * math.pi / image_rows
    )
    scale = 1.0 / math.sqrt(samples)
    return jnp.concatenate([jnp.cos(phase) * scale, jnp.sin(phase) * scale], axis=0).astype(
        jnp.bfloat16
    )


def apply_phase(mixed, offsets, sample_index):
    angle = jnp.mod(offsets[:, None] * (sample_index[None, :] - KR // 2), ROWS).astype(
        jnp.float32
    ) * (2.0 * math.pi / ROWS)
    cosine = jnp.cos(angle)[:, :, None]
    sine = jnp.sin(angle)[:, :, None]
    real_part = mixed[:, :, :COLS]
    imag_part = mixed[:, :, COLS:]
    return jnp.concatenate(
        [real_part * cosine - imag_part * sine, real_part * sine + imag_part * cosine], axis=2
    ).astype(jnp.bfloat16)


def window_mask(block_offset, count):
    target = np.arange(count)[:, None]
    source = np.arange(count)[None, :]
    distance = block_offset * count + source - target
    return ((distance >= 0) & (distance < WIN)).astype(np.float32)


def combine_parts(product, strip_rows):
    product = lax.optimization_barrier(product)
    real_part = product[:, :strip_rows, :COLS] - product[:, strip_rows:, COLS:]
    imag_part = product[:, :strip_rows, COLS:] + product[:, strip_rows:, :COLS]
    return jnp.concatenate([real_part, imag_part], axis=2)


def remove_background(stack):
    frame_count = stack.shape[0]
    series = jnp.transpose(stack, (1, 2, 0))
    source = jnp.arange(frame_count, dtype=jnp.int32)[:, None]
    target = jnp.arange(frame_count, dtype=jnp.int32)[None, :]
    behind = jnp.where(jnp.mod(target - source, frame_count) < BG, 1.0 / BG, 0.0).astype(
        jnp.float32
    )
    weights = jnp.where(source == target, 1.0, 0.0).astype(jnp.float32) - behind
    return jnp.einsum("rcg,gf->rcf", series, weights, precision=lax.Precision.HIGHEST)


def body(spectra, offsets):
    sub_dev = spectra.shape[0]
    strip_rows = ROWS // lax.axis_size("strip")
    first_row = lax.axis_index("strip") * strip_rows
    own_rows = first_row + jnp.arange(strip_rows, dtype=jnp.int32)
    columns = column_table(spectra.shape[2] // 2, COLS)
    table = row_table(own_rows, KR, ROWS)
    passes = (WIN - 2 + sub_dev) // sub_dev
    piece = lax.all_gather(spectra, "strip", axis=1, tiled=True)
    sample_index = jnp.arange(piece.shape[1], dtype=jnp.int32)
    shifted = apply_phase(
        jnp.einsum("skc,cn->skn", piece, columns, preferred_element_type=jnp.float32),
        offsets,
        sample_index,
    )
    product = jnp.einsum("mk,skn->smn", table, shifted, preferred_element_type=jnp.float32)
    images = combine_parts(product, strip_rows)
    frames = jnp.einsum(
        "ab,bmn->amn", jnp.asarray(window_mask(0, sub_dev)), images, precision=lax.Precision.HIGHEST
    )
    moving = images
    for block_offset in range(1, passes + 1):
        moving = from_behind(moving, "sub", -1)
        frames = frames + jnp.einsum(
            "ab,bmn->amn",
            jnp.asarray(window_mask(block_offset, sub_dev)),
            moving,
            precision=lax.Precision.HIGHEST,
        )
    real_part = frames[:, :, :COLS]
    imag_part = frames[:, :, COLS:]
    log_power = jnp.log(1.0 + real_part * real_part + imag_part * imag_part)
    padded = extended(log_power, (("strip", 1),), 1)
    padded = jnp.pad(padded, ((0, 0), (0, 0), (1, 1)))
    total = jnp.zeros_like(log_power)
    for row_step in range(3):
        for col_step in range(3):
            total = total + padded[:, row_step : row_step + strip_rows, col_step : col_step + COLS]
    filtered = total / 9.0
    return remove_background(
        lax.all_to_all(filtered, "sub", split_axis=2, concat_axis=0, tiled=True)
    )


def solution(mesh):
    in_specs = (P("sub", "strip", None), P("sub"))
    out_specs = P("strip", "sub", None)
    return jax.shard_map(body, mesh=mesh, in_specs=in_specs, out_specs=out_specs, check_vma=False)
```

profile of v0, /device:TPU:1, one launch (start us, length us, event | category | flops | bytes accessed | tf_op | source)
XLA Modules:
  0.0 272.1 jit_solution(287190779689159328)
XLA Ops:
  6.5 0.0 all-gather.2.cloned.1.call-start
  6.5 0.7 all-gather.2.cloned.1.call-update
  7.3 4.0 %fusion.15 = bf16[1024,256]{0,1:T(8,128)(2,1)S(1)} fusion(), kind=kLoop, calls=%fused_computation.27 | loop fusion | flops 4456448 | bytes 524288 | tf_op jit(solution)/shard_map/convert.9
  11.2 4.3 %negate_convert_fusion = (bf16[1024,256]{0,1:T(8,128)(2,1)S(1)}, bf16[1024,256]{0,1:T(8,128)(2,1)S(1)}) fusion(), kind=kLoop, calls=%fused_computation.21 | loop fusion | flops 5242880 | bytes 1048576 | tf_op jit(solution)/shard_map/convert.6
  15.6 0.8 fusion.55
  16.4 0.6 multiply_convert_fusion.2
  17.0 115.6 %all-gather.2.cloned.1.call-done = bf16[2,256,2048]{2,1,0:T(8,128)(2,1)} async-done(((bf16[2,32,2048]{2,1,0:T(8,128)(2,1)}), bf16[2,256,2048]{2,1,0:T(8,128)(2,1)}) %all-gather.2.cloned.1.call-update) | async-done | bytes 2097168 | tf_op jit(solution)/shard_map/all_gather | solution.py:105
  132.6 2.9 %fusion.7 = f32[2,256,512]{1,2,0:T(8,128)S(1)} fusion(bf16[2,256,2048]{2,1,0:T(8,128)(2,1)} %all-gather.2.cloned.1.call-done, bf16[1024,256]{0,1:T(8,128)(2,1)S(1)} %get-tuple-element.16, bf16[1024,256]{0,1:T(8,128)(2,1)S(1)} %get-tuple-element.15, bf16[1024,256]{0,1:T(8,128)(2,1)S(1)} %fusion.15), kind=kOutput, calls=%fused_computation.11 | convolution fusion | flops 1082130432 | bytes 4718592 | tf_op jit(solution)/shard_map/skc,cn->skn/dot_general | solution.py:108
  135.5 0.1 subtract_convert_fusion
  135.6 0.3 convolution_bitcast_fusion
  136.0 0.0 copy-start
  136.0 0.1 slice_subtract_fusion
  136.1 4.1 %collective-permute-start = (f32[2,128,512]{1,2,0:T(8,128)S(1)}, f32[2,128,512]{1,2,0:T(8,128)S(1)}, u32[]{:S(2)}, u32[]{:S(2)}) collective-permute-start(f32[2,128,512]{1,2,0:T(8,128)S(1)} %pad_maximum_fusion), channel_id=1, source_target_pairs={{0,504},{8,0},{16,8},{24,16},{32,24},{40,32},{48,40},{56,48},{64,5... | collective-permute-start | bytes 1572872 | tf_op jit(solution)/shard_map/ppermute | solution.py:18
  140.2 6.4 %collective-permute-done = f32[2,128,512]{1,2,0:T(8,128)S(1)} collective-permute-done((f32[2,128,512]{1,2,0:T(8,128)S(1)}, f32[2,128,512]{1,2,0:T(8,128)S(1)}, u32[]{:S(2)}, u32[]{:S(2)}) %collective-permute-start) | collective-permute-done | bytes 524320 | tf_op jit(solution)/shard_map/ppermute | solution.py:18
  146.6 3.4 %collective-permute-start.1 = (f32[2,128,512]{1,2,0:T(8,128)S(1)}, f32[2,128,512]{1,2,0:T(8,128)S(1)}, u32[]{:S(2)}, u32[]{:S(2)}) collective-permute-start(f32[2,128,512]{1,2,0:T(8,128)S(1)} %collective-permute-done), channel_id=1, source_target_pairs={{0,504},{8,0},{16,8},{24,16},{32,24},{40,32},{48,40},{56,48},{64,5... | collective-permute-start | bytes 1572872 | tf_op jit(solution)/shard_map/ppermute | solution.py:18
  150.0 7.1 %collective-permute-done.1 = f32[2,128,512]{1,2,0:T(8,128)S(1)} collective-permute-done((f32[2,128,512]{1,2,0:T(8,128)S(1)}, f32[2,128,512]{1,2,0:T(8,128)S(1)}, u32[]{:S(2)}, u32[]{:S(2)}) %collective-permute-start.1) | collective-permute-done | bytes 524320 | tf_op jit(solution)/shard_map/ppermute | solution.py:18
  157.1 12.1 %collective-permute-start.2 = (f32[2,128,512]{1,2,0:T(8,128)S(1)}, f32[2,128,512]{1,2,0:T(8,128)S(1)}, u32[]{:S(2)}, u32[]{:S(2)}) collective-permute-start(f32[2,128,512]{1,2,0:T(8,128)S(1)} %collective-permute-done.1), channel_id=1, source_target_pairs={{0,504},{8,0},{16,8},{24,16},{32,24},{40,32},{48,40},{56,48},{64,5... | collective-permute-start | bytes 1572872 | tf_op jit(solution)/shard_map/ppermute | solution.py:18
  169.2 0.2 copy.34
  169.4 0.0 copy-done
  169.4 1.9 fusion.72
  171.3 0.2 copy.35
  171.6 2.0 convolution_add_fusion.3
  173.6 0.2 copy.36
  173.8 0.0 collective-permute-done.2
  173.9 14.7 %collective-permute-start.3 = (f32[2,128,512]{1,2,0:T(8,128)S(1)}, f32[2,128,512]{1,2,0:T(8,128)S(1)}, u32[]{:S(2)}, u32[]{:S(2)}) collective-permute-start(f32[2,128,512]{1,2,0:T(8,128)S(1)} %collective-permute-done.2), channel_id=1, source_target_pairs={{0,504},{8,0},{16,8},{24,16},{32,24},{40,32},{48,40},{56,48},{64,5... | collective-permute-start | bytes 1572872 | tf_op jit(solution)/shard_map/ppermute | solution.py:18
  188.6 2.0 convolution_add_fusion.2
  190.6 0.0 copy-start.1
  190.6 0.2 copy.37
  190.8 2.0 convolution_add_fusion.1
  192.9 0.0 collective-permute-done.3
  192.9 0.2 copy.38
  193.1 0.0 copy-done.1
  193.1 2.0 fusion.8
  195.2 0.2 fusion.24
  195.4 8.6 %collective-permute-start.4 = (f32[2,1,256]{2,0,1:T(2,128)S(1)}, f32[2,1,256]{2,0,1:T(2,128)S(1)}, u32[]{:S(2)}, u32[]{:S(2)}) collective-permute-start(f32[2,1,256]{2,0,1:T(2,128)S(1)} %get-tuple-element.9), channel_id=1, source_target_pairs={{0,1},{1,2},{2,3},{3,4},{4,5},{5,6},{6,7},{8,9},{9,10},{10,11},{11... | collective-permute-start | bytes 6152 | tf_op jit(solution)/shard_map/ppermute | solution.py:28
  204.0 1.3 collective-permute-start.5
  205.3 0.0 collective-permute-done.4
  205.3 11.7 %collective-permute-done.5 = f32[2,1,256]{2,0,1:T(2,128)S(1)} collective-permute-done((f32[2,1,256]{2,0,1:T(2,128)S(1)}, f32[2,1,256]{2,0,1:T(2,128)S(1)}, u32[]{:S(2)}, u32[]{:S(2)}) %collective-permute-start.5) | collective-permute-done | bytes 2080 | tf_op jit(solution)/shard_map/ppermute | solution.py:29
  217.0 0.5 select_maximum_fusion
  217.5 1.0 fusion.19
  218.4 0.2 copy.39
  218.6 45.0 %all_to_all.18 = f32[2,128,256]{1,0,2:T(2,128)S(1)} all-to-all(f32[2,128,256]{1,0,2:T(2,128)S(1)} %copy.39), channel_id=1, replica_groups=mesh['sub'=64,'strip'=8] {'sub'}, dimensions={2} | all-to-all | bytes 524288 | tf_op jit(solution)/shard_map/all_to_all | solution.py:137
  263.6 0.2 copy.41
  263.9 0.1 copy.42
  264.0 0.4 fusion.26
  264.4 0.9 copy.43
  (5 shorter events, 0.1 us)
Async XLA Ops:
  6.5 126.1 %all-gather.2.cloned.1.call-start = ((), (), s32[]{:S(2)}) async-start(), calls=%async_computation.1 | async-start | bytes 2359296 | tf_op jit(solution)/shard_map/all_gather | solution.py:105
  136.0 33.5 %copy-start = (f32[2,2,1]{1,0,2:T(2,128)S(1)}, f32[2,2,1]{1,0,2:T(2,128)}, u32[]{:S(2)}) copy-start(f32[2,2,1]{1,0,2:T(2,128)} %constant.88) | copy-start | bytes 52
  136.1 10.5 %collective-permute-start = (f32[2,128,512]{1,2,0:T(8,128)S(1)}, f32[2,128,512]{1,2,0:T(8,128)S(1)}, u32[]{:S(2)}, u32[]{:S(2)}) collective-permute-start(f32[2,128,512]{1,2,0:T(8,128)S(1)} %pad_maximum_fusion), channel_id=1, source_target_pairs={{0,504},{8,0},{16,8},{24,16},{32,24},{40,32},{48,40},{56,48},{64,5... | collective-permute-start | bytes 1572872 | tf_op jit(solution)/shard_map/ppermute | solution.py:18
  146.6 10.5 %collective-permute-start.1 = (f32[2,128,512]{1,2,0:T(8,128)S(1)}, f32[2,128,512]{1,2,0:T(8,128)S(1)}, u32[]{:S(2)}, u32[]{:S(2)}) collective-permute-start(f32[2,128,512]{1,2,0:T(8,128)S(1)} %collective-permute-done), channel_id=1, source_target_pairs={{0,504},{8,0},{16,8},{24,16},{32,24},{40,32},{48,40},{56,48},{64,5... | collective-permute-start | bytes 1572872 | tf_op jit(solution)/shard_map/ppermute | solution.py:18
  157.1 16.8 %collective-permute-start.2 = (f32[2,128,512]{1,2,0:T(8,128)S(1)}, f32[2,128,512]{1,2,0:T(8,128)S(1)}, u32[]{:S(2)}, u32[]{:S(2)}) collective-permute-start(f32[2,128,512]{1,2,0:T(8,128)S(1)} %collective-permute-done.1), channel_id=1, source_target_pairs={{0,504},{8,0},{16,8},{24,16},{32,24},{40,32},{48,40},{56,48},{64,5... | collective-permute-start | bytes 1572872 | tf_op jit(solution)/shard_map/ppermute | solution.py:18
  173.9 19.0 %collective-permute-start.3 = (f32[2,128,512]{1,2,0:T(8,128)S(1)}, f32[2,128,512]{1,2,0:T(8,128)S(1)}, u32[]{:S(2)}, u32[]{:S(2)}) collective-permute-start(f32[2,128,512]{1,2,0:T(8,128)S(1)} %collective-permute-done.2), channel_id=1, source_target_pairs={{0,504},{8,0},{16,8},{24,16},{32,24},{40,32},{48,40},{56,48},{64,5... | collective-permute-start | bytes 1572872 | tf_op jit(solution)/shard_map/ppermute | solution.py:18
  190.6 2.5 copy-start.1
  195.4 9.9 %collective-permute-start.4 = (f32[2,1,256]{2,0,1:T(2,128)S(1)}, f32[2,1,256]{2,0,1:T(2,128)S(1)}, u32[]{:S(2)}, u32[]{:S(2)}) collective-permute-start(f32[2,1,256]{2,0,1:T(2,128)S(1)} %get-tuple-element.9), channel_id=1, source_target_pairs={{0,1},{1,2},{2,3},{3,4},{4,5},{5,6},{6,7},{8,9},{9,10},{10,11},{11... | collective-permute-start | bytes 6152 | tf_op jit(solution)/shard_map/ppermute | solution.py:28
  204.0 13.0 %collective-permute-start.5 = (f32[2,1,256]{2,0,1:T(2,128)S(1)}, f32[2,1,256]{2,0,1:T(2,128)S(1)}, u32[]{:S(2)}, u32[]{:S(2)}) collective-permute-start(f32[2,1,256]{2,0,1:T(2,128)S(1)} %get-tuple-element.10), channel_id=1, source_target_pairs={{1,0},{2,1},{3,2},{4,3},{5,4},{6,5},{7,6},{9,8},{10,9},{11,10},{12... | collective-permute-start | bytes 6152 | tf_op jit(solution)/shard_map/ppermute | solution.py:29
Sparse Core Ops, SparseCore 0:
  10.6 121.9 all-gather.1
where the time goes:
time: 272 us
  waiting for transfers between devices  141 us (52%)
  blocking collectives  45 us (17%)
  starting transfers between devices  44.2 us (16%)
  between operations  13.7 us (5%)
  matrix products  13.6 us (5%)
  other arithmetic  11.6 us (4%)
    all_gather x1, waiting for transfers between devices, body(): piece = lax.all_gather(spectra, 'strip', axis=1, tiled=True)  116 us
    all_to_all x1, blocking collectives, body(): lax.all_to_all(filtered, 'sub', split_axis=2, concat_axis=0, tiled=True)  45 us
    ppermute x4, starting transfers between devices, from_behind(): return lax.ppermute(value, axis, pairs)  34.3 us
    ppermute x4, waiting for transfers between devices, from_behind(): return lax.ppermute(value, axis, pairs)  13.5 us
    ppermute x1, waiting for transfers between devices, extended(): after = lax.ppermute(leading, axis, down)  11.7 us
    another operation x4, other arithmetic  9.06 us
    ppermute x1, starting transfers between devices, extended(): before = lax.ppermute(last, axis, up)  8.55 us
    dot_general x4, matrix products, body(): jnp.einsum('ab,bmn->amn', jnp.asarray(window_mask(block_offset, sub_dev))...  8.05 us
  transfers between devices with their start and end apart: 7, of which 4 were waited for; matrix products, arithmetic and copies ran while one was open for 7% of the time, Pallas kernels for 0%

commit v1 on v0

--- a/solution.py
+++ b/solution.py
@@ -4,6 +4,7 @@
 import numpy as np
 from jax import lax
 from jax.sharding import PartitionSpec as P
+from jax.lax import all_to_all, axis_size
 
 KR = 256
 ROWS = 1024
@@ -102,7 +103,10 @@
     columns = column_table(spectra.shape[2] // 2, COLS)
     table = row_table(own_rows, KR, ROWS)
     passes = (WIN - 2 + sub_dev) // sub_dev
-    piece = lax.all_gather(spectra, "strip", axis=1, tiled=True)
+    base_arr = axis_size("strip")
+    p_next = jnp.stack([spectra] * base_arr)
+    res = all_to_all(p_next, axis_name="strip", split_axis=0, concat_axis=0)
+    piece = jnp.concatenate(res, 1)
     sample_index = jnp.arange(piece.shape[1], dtype=jnp.int32)
     shifted = apply_phase(
         jnp.einsum("skc,cn->skn", piece, columns, preferred_element_type=jnp.float32),

time: 272 us -> 235 us (0.86)
  waiting for transfers between devices: 141 us -> 49.5 us
  starting transfers between devices: 44.2 us -> 110 us
  between operations: 13.7 us -> 0.31 us
  local copies, waits for them, and re-layouts: 2.56 us -> 6.14 us
    all_gather x1 -> x0, waiting for transfers between devices: 116 us -> none  [body(): piece = lax.all_gather(spectra, 'strip', axis=1, tiled=True)]
    ppermute x4, starting transfers between devices: 34.3 us -> 78.1 us  [from_behind(): return lax.ppermute(value, axis, pairs)]
    all_to_all x0 -> x1, waiting for transfers between devices: none -> 39.2 us  [body(): res = all_to_all(p_next, axis_name='strip', split_axis=0, concat_axis=0)]
    all_to_all x0 -> x1, starting transfers between devices: none -> 18.2 us  [body(): res = all_to_all(p_next, axis_name='strip', split_axis=0, concat_axis=0)]
    ppermute x1, waiting for transfers between devices: 11.7 us -> 0.01 us  [extended(): after = lax.ppermute(leading, axis, down)]
    ppermute x1, starting transfers between devices: 8.55 us -> 12.7 us  [extended(): before = lax.ppermute(last, axis, up)]
    ppermute x4, waiting for transfers between devices: 13.5 us -> 9.55 us  [from_behind(): return lax.ppermute(value, axis, pairs)]
  transfers between devices with their start and end apart: 7 -> 7, of which waited for: 4 -> 4; matrix products, arithmetic and copies ran while one was open for 7% -> 8% of each run, Pallas kernels for 0% -> 0%
where the time goes in v1:
time: 235 us
  starting transfers between devices  110 us (47%)
  waiting for transfers between devices  49.5 us (21%)
  blocking collectives  45 us (19%)
  other arithmetic  11.8 us (5%)
  matrix products  11.8 us (5%)
  local copies, waits for them, and re-layouts  6.14 us (3%)
    ppermute x4, starting transfers between devices, from_behind(): return lax.ppermute(value, axis, pairs)  78.1 us
    all_to_all x1, blocking collectives, body(): lax.all_to_all(filtered, 'sub', split_axis=2, concat_axis=0, tiled=True)  45 us
    all_to_all x1, waiting for transfers between devices, body(): res = all_to_all(p_next, axis_name='strip', split_axis=0, concat_axis=0)  39.2 us
    all_to_all x1, starting transfers between devices, body(): res = all_to_all(p_next, axis_name='strip', split_axis=0, concat_axis=0)  18.2 us
    ppermute x1, starting transfers between devices, extended(): before = lax.ppermute(last, axis, up)  12.7 us
    another operation x4, other arithmetic  9.91 us
    ppermute x4, waiting for transfers between devices, from_behind(): return lax.ppermute(value, axis, pairs)  9.55 us
    dot_general x4, matrix products, body(): jnp.einsum('ab,bmn->amn', jnp.asarray(window_mask(block_offset, sub_dev))...  7.93 us
  transfers between devices with their start and end apart: 7, of which 4 were waited for; matrix products, arithmetic and copies ran while one was open for 8% of the time, Pallas kernels for 0%

profile of v1, /device:TPU:1, one launch (start us, length us, event | category | flops | bytes accessed | tf_op | source)
XLA Modules:
  0.0 235.0 jit_solution(6658816487928637441)
XLA Ops:
  0.0 2.5 %stack.2 = bf16[8,2,32,2048]{3,2,1,0:T(8,128)(2,1)} broadcast(bf16[2,32,2048]{2,1,0:T(8,128)(2,1)} %param.7), dimensions={1,2,3} | broadcast | bytes 2359296 | tf_op jit(solution)/shard_map/stack | solution.py:107
  2.5 18.2 %all-to-all-start = ((bf16[8,2,32,2048]{3,2,1,0:T(8,128)(2,1)}), bf16[8,2,32,2048]{3,2,1,0:T(8,128)(2,1)S(1)}, u32[]{:S(2)}, u32[]{:S(2)}) async-start(bf16[8,2,32,2048]{3,2,1,0:T(8,128)(2,1)} %stack.2), calls=%async_computation | async-start | bytes 4194304 | tf_op jit(solution)/shard_map/all_to_all | solution.py:108
  20.8 4.0 %fusion.15 = bf16[1024,256]{0,1:T(8,128)(2,1)S(1)} fusion(), kind=kLoop, calls=%fused_computation.27 | loop fusion | flops 4456448 | bytes 524288 | tf_op jit(solution)/shard_map/convert.9
  24.8 5.2 %negate_convert_fusion = (bf16[1024,256]{0,1:T(8,128)(2,1)S(1)}, bf16[1024,256]{0,1:T(8,128)(2,1)}) fusion(), kind=kLoop, calls=%fused_computation.21 | loop fusion | flops 5242880 | bytes 1048576 | tf_op jit(solution)/shard_map/convert.6
  30.0 0.0 copy-done.2
  30.0 0.1 fusion.55
  30.1 0.6 multiply_convert_fusion.2
  30.7 39.2 %all-to-all-done = bf16[8,2,32,2048]{3,2,1,0:T(8,128)(2,1)S(1)} async-done(((bf16[8,2,32,2048]{3,2,1,0:T(8,128)(2,1)}), bf16[8,2,32,2048]{3,2,1,0:T(8,128)(2,1)S(1)}, u32[]{:S(2)}, u32[]{:S(2)}) %all-to-all-start) | async-done | bytes 2097184 | tf_op jit(solution)/shard_map/all_to_all | solution.py:108
  70.0 0.2 copy.35
  70.2 0.8 copy-done
  71.0 1.3 fusion.7
  72.3 0.1 subtract_convert_fusion
  72.4 0.3 convolution_bitcast_fusion
  72.8 0.0 copy-start.1
  72.8 0.1 slice_subtract_fusion
  72.9 3.8 %collective-permute-start = (f32[2,128,512]{1,2,0:T(8,128)S(1)}, f32[2,128,512]{1,2,0:T(8,128)S(1)}, u32[]{:S(2)}, u32[]{:S(2)}) collective-permute-start(f32[2,128,512]{1,2,0:T(8,128)S(1)} %pad_maximum_fusion), channel_id=1, source_target_pairs={{0,504},{8,0},{16,8},{24,16},{32,24},{40,32},{48,40},{56,48},{64,5... | collective-permute-start | bytes 1572872 | tf_op jit(solution)/shard_map/ppermute | solution.py:19
  76.7 8.0 %collective-permute-done = f32[2,128,512]{1,2,0:T(8,128)S(1)} collective-permute-done((f32[2,128,512]{1,2,0:T(8,128)S(1)}, f32[2,128,512]{1,2,0:T(8,128)S(1)}, u32[]{:S(2)}, u32[]{:S(2)}) %collective-permute-start) | collective-permute-done | bytes 524320 | tf_op jit(solution)/shard_map/ppermute | solution.py:19
  84.7 41.0 %collective-permute-start.1 = (f32[2,128,512]{1,2,0:T(8,128)S(1)}, f32[2,128,512]{1,2,0:T(8,128)S(1)}, u32[]{:S(2)}, u32[]{:S(2)}) collective-permute-start(f32[2,128,512]{1,2,0:T(8,128)S(1)} %collective-permute-done), channel_id=1, source_target_pairs={{0,504},{8,0},{16,8},{24,16},{32,24},{40,32},{48,40},{56,48},{64,5... | collective-permute-start | bytes 1572872 | tf_op jit(solution)/shard_map/ppermute | solution.py:19
  125.7 1.5 collective-permute-done.1
  127.2 18.6 %collective-permute-start.2 = (f32[2,128,512]{1,2,0:T(8,128)S(1)}, f32[2,128,512]{1,2,0:T(8,128)S(1)}, u32[]{:S(2)}, u32[]{:S(2)}) collective-permute-start(f32[2,128,512]{1,2,0:T(8,128)S(1)} %collective-permute-done.1), channel_id=1, source_target_pairs={{0,504},{8,0},{16,8},{24,16},{32,24},{40,32},{48,40},{56,48},{64,5... | collective-permute-start | bytes 1572872 | tf_op jit(solution)/shard_map/ppermute | solution.py:19
  145.8 0.2 copy.36
  146.1 0.0 copy-done.1
  146.1 1.9 fusion.72
  148.0 0.2 copy.37
  148.2 1.9 convolution_add_fusion.3
  150.2 0.2 copy.38
  150.4 0.0 collective-permute-done.2
  150.4 14.8 %collective-permute-start.3 = (f32[2,128,512]{1,2,0:T(8,128)S(1)}, f32[2,128,512]{1,2,0:T(8,128)S(1)}, u32[]{:S(2)}, u32[]{:S(2)}) collective-permute-start(f32[2,128,512]{1,2,0:T(8,128)S(1)} %collective-permute-done.2), channel_id=1, source_target_pairs={{0,504},{8,0},{16,8},{24,16},{32,24},{40,32},{48,40},{56,48},{64,5... | collective-permute-start | bytes 1572872 | tf_op jit(solution)/shard_map/ppermute | solution.py:19
  165.2 1.9 convolution_add_fusion.2
  167.2 0.0 copy-start.3
  167.2 0.2 copy.39
  167.4 2.0 convolution_add_fusion.1
  169.4 0.0 collective-permute-done.3
  169.4 0.2 copy.40
  169.7 2.0 fusion.8
  171.7 0.2 fusion.24
  172.0 1.3 collective-permute-start.5
  173.3 12.7 %collective-permute-start.4 = (f32[2,1,256]{2,0,1:T(2,128)S(1)}, f32[2,1,256]{2,0,1:T(2,128)S(1)}, u32[]{:S(2)}, u32[]{:S(2)}) collective-permute-start(f32[2,1,256]{2,0,1:T(2,128)S(1)} %get-tuple-element.9), channel_id=1, source_target_pairs={{0,1},{1,2},{2,3},{3,4},{4,5},{5,6},{6,7},{8,9},{9,10},{10,11},{11... | collective-permute-start | bytes 6152 | tf_op jit(solution)/shard_map/ppermute | solution.py:29
  186.0 0.0 collective-permute-done.5
  186.0 0.7 collective-permute-done.4
  186.7 0.5 select_maximum_fusion
  187.2 1.0 fusion.19
  188.1 0.2 copy.41
  188.3 45.0 %all_to_all.23 = f32[2,128,256]{1,0,2:T(2,128)S(1)} all-to-all(f32[2,128,256]{1,0,2:T(2,128)S(1)} %copy.41), channel_id=1, replica_groups=mesh['sub'=64,'strip'=8] {'sub'}, dimensions={2} | all-to-all | bytes 524288 | tf_op jit(solution)/shard_map/all_to_all | solution.py:141
  233.3 0.2 copy.43
  233.5 0.1 copy.44
  233.7 0.4 fusion.26
  234.1 0.9 copy.45
  (8 shorter events, 0.1 us)
Async XLA Ops:
  2.5 27.4 %copy-start.2 = (s32[2]{0:T(128)S(1)}, s32[2]{0:T(128)}, u32[]{:S(2)}) copy-start(s32[2]{0:T(128)} %param.8) | copy-start | bytes 28
  2.5 67.4 %all-to-all-start = ((bf16[8,2,32,2048]{3,2,1,0:T(8,128)(2,1)}), bf16[8,2,32,2048]{3,2,1,0:T(8,128)(2,1)S(1)}, u32[]{:S(2)}, u32[]{:S(2)}) async-start(bf16[8,2,32,2048]{3,2,1,0:T(8,128)(2,1)} %stack.2), calls=%async_computation | async-start | bytes 4194304 | tf_op jit(solution)/shard_map/all_to_all | solution.py:108
  70.0 1.0 copy-start
  72.8 73.3 %copy-start.1 = (f32[2,2,1]{1,0,2:T(2,128)S(1)}, f32[2,2,1]{1,0,2:T(2,128)}, u32[]{:S(2)}) copy-start(f32[2,2,1]{1,0,2:T(2,128)} %constant.88) | copy-start | bytes 52
  72.9 11.8 %collective-permute-start = (f32[2,128,512]{1,2,0:T(8,128)S(1)}, f32[2,128,512]{1,2,0:T(8,128)S(1)}, u32[]{:S(2)}, u32[]{:S(2)}) collective-permute-start(f32[2,128,512]{1,2,0:T(8,128)S(1)} %pad_maximum_fusion), channel_id=1, source_target_pairs={{0,504},{8,0},{16,8},{24,16},{32,24},{40,32},{48,40},{56,48},{64,5... | collective-permute-start | bytes 1572872 | tf_op jit(solution)/shard_map/ppermute | solution.py:19
  84.7 42.5 %collective-permute-start.1 = (f32[2,128,512]{1,2,0:T(8,128)S(1)}, f32[2,128,512]{1,2,0:T(8,128)S(1)}, u32[]{:S(2)}, u32[]{:S(2)}) collective-permute-start(f32[2,128,512]{1,2,0:T(8,128)S(1)} %collective-permute-done), channel_id=1, source_target_pairs={{0,504},{8,0},{16,8},{24,16},{32,24},{40,32},{48,40},{56,48},{64,5... | collective-permute-start | bytes 1572872 | tf_op jit(solution)/shard_map/ppermute | solution.py:19
  127.2 23.2 %collective-permute-start.2 = (f32[2,128,512]{1,2,0:T(8,128)S(1)}, f32[2,128,512]{1,2,0:T(8,128)S(1)}, u32[]{:S(2)}, u32[]{:S(2)}) collective-permute-start(f32[2,128,512]{1,2,0:T(8,128)S(1)} %collective-permute-done.1), channel_id=1, source_target_pairs={{0,504},{8,0},{16,8},{24,16},{32,24},{40,32},{48,40},{56,48},{64,5... | collective-permute-start | bytes 1572872 | tf_op jit(solution)/shard_map/ppermute | solution.py:19
  150.4 19.0 %collective-permute-start.3 = (f32[2,128,512]{1,2,0:T(8,128)S(1)}, f32[2,128,512]{1,2,0:T(8,128)S(1)}, u32[]{:S(2)}, u32[]{:S(2)}) collective-permute-start(f32[2,128,512]{1,2,0:T(8,128)S(1)} %collective-permute-done.2), channel_id=1, source_target_pairs={{0,504},{8,0},{16,8},{24,16},{32,24},{40,32},{48,40},{56,48},{64,5... | collective-permute-start | bytes 1572872 | tf_op jit(solution)/shard_map/ppermute | solution.py:19
  167.2 2.5 %copy-start.3 = (f32[2,2,1]{1,0,2:T(2,128)S(1)}, f32[2,2,1]{1,0,2:T(2,128)}, u32[]{:S(2)}) copy-start(f32[2,2,1]{1,0,2:T(2,128)} %constant.89) | copy-start | bytes 52
  172.0 14.0 %collective-permute-start.5 = (f32[2,1,256]{2,0,1:T(2,128)S(1)}, f32[2,1,256]{2,0,1:T(2,128)S(1)}, u32[]{:S(2)}, u32[]{:S(2)}) collective-permute-start(f32[2,1,256]{2,0,1:T(2,128)S(1)} %get-tuple-element.10), channel_id=1, source_target_pairs={{1,0},{2,1},{3,2},{4,3},{5,4},{6,5},{7,6},{9,8},{10,9},{11,10},{12... | collective-permute-start | bytes 6152 | tf_op jit(solution)/shard_map/ppermute | solution.py:30
  173.3 13.4 %collective-permute-start.4 = (f32[2,1,256]{2,0,1:T(2,128)S(1)}, f32[2,1,256]{2,0,1:T(2,128)S(1)}, u32[]{:S(2)}, u32[]{:S(2)}) collective-permute-start(f32[2,1,256]{2,0,1:T(2,128)S(1)} %get-tuple-element.9), channel_id=1, source_target_pairs={{0,1},{1,2},{2,3},{3,4},{4,5},{5,6},{6,7},{8,9},{9,10},{10,11},{11... | collective-permute-start | bytes 6152 | tf_op jit(solution)/shard_map/ppermute | solution.py:29
